TPU v7x, 32 devices: a whole 2x2x4 slice. The times are simulated.
32 devices in a mesh: groups: 2 (over x), rows: 16 (over z, y, core).
Axes of the slice: x: 2, y: 2, z: 4, core: 2. Of those that a mesh axis runs over, the one named last changes fastest.
Arguments:
- pair: bfloat16 [512, 256, 128], P(('groups', 'rows')), parts along dimension 0, may hold values from -6 to 6
- proj_weights: bfloat16 [6, 128, 128], replicated, may hold values from -0.5 to 0.5
- cotangent: bfloat16 [512, 256, 128], P(('groups', 'rows')), parts along dimension 0, may hold values from -8.5 to 8.5
Outputs:
- update: bfloat16 [512, 256, 128], P(('groups', 'rows')), parts along dimension 0
- pair_grad: bfloat16 [512, 256, 128], P(('groups', 'rows')), parts along dimension 0
- weight_grads: float32 [12, 128, 128], P('groups'), parts along dimension 0
There are 2 independent parts, one for each index of `groups`. A program takes and returns all parts, laid end to end along the dimension named above; an argument that names none is the same for every part. Nothing has to cross between parts.
All inputs are finite; a program needn't handle non-finite values.
Results may differ from a plain program's by a relative error of at most 0.015.
Values may be sent and summed in bfloat16 or wider, within the bound.
A program may use at most 128 MiB of HBM per device.

v0:
```python
import jax
import jax.numpy as jnp
from jax import lax
from jax.sharding import PartitionSpec as P


def layer_norm(values, along_dim):
    centred = values - jnp.mean(values, axis=along_dim, keepdims=True)
    inv_scale = lax.rsqrt(jnp.mean(centred * centred, axis=along_dim, keepdims=True) + 1e-05)
    return (centred * inv_scale, inv_scale)


def norm_backward(normed, inv_scale, upstream, along_dim):
    return (
        upstream
        - jnp.mean(upstream, axis=along_dim, keepdims=True)
        - normed * jnp.mean(upstream * normed, axis=along_dim, keepdims=True)
    ) * inv_scale


def triangle_slab(pieces):
    left_slab, right_slab = pieces
    product = lax.dot_general(
        left_slab, right_slab, (((3,), (3,)), ((0, 1), (0, 1))), preferred_element_type=jnp.float32
    )
    return (product.astype(jnp.bfloat16), left_slab, right_slab)


def edge_backward(upstream, left_slab, right_slab):
    left_part = lax.dot_general(
        upstream, right_slab, (((3,), (2,)), ((0, 1), (0, 1))), preferred_element_type=jnp.float32
    )
    right_part = lax.dot_general(
        upstream, left_slab, (((2,), (2,)), ((0, 1), (0, 1))), preferred_element_type=jnp.float32
    )
    return (left_part.astype(jnp.bfloat16), right_part.astype(jnp.bfloat16))


def body(pair, proj_weights, cotangent):
    residues = pair.shape[1]
    local_rows = pair.shape[0]
    chans = pair.shape[2]
    ranks = lax.axis_size("rows")
    slab_width = chans // ranks
    normed_in, scale_in = layer_norm(pair.astype(jnp.float32), 2)
    normed_bf = normed_in.astype(jnp.bfloat16)
    edge_pre = jnp.einsum(
        "ikd,ndc->ncik", normed_bf, proj_weights[0:4], preferred_element_type=jnp.float32
    )
    gate_pre = jnp.einsum(
        "ikd,dc->ikc", normed_bf, proj_weights[4], preferred_element_type=jnp.float32
    )
    left_sig = jax.nn.sigmoid(edge_pre[1])
    right_sig = jax.nn.sigmoid(edge_pre[3])
    left_edge = (
        (left_sig * edge_pre[0])
        .astype(jnp.bfloat16)
        .reshape(ranks, slab_width, local_rows, residues)
    )
    right_edge = (
        (right_sig * edge_pre[2])
        .astype(jnp.bfloat16)
        .reshape(ranks, slab_width, local_rows, residues)
    )
    products, left_held, right_held = triangle_slab(
        (
            lax.all_to_all(left_edge, "rows", split_axis=0, concat_axis=2, tiled=True),
            lax.all_to_all(right_edge, "rows", split_axis=0, concat_axis=2, tiled=True),
        )
    )
    regrouped = lax.all_to_all(products, "rows", split_axis=2, concat_axis=0, tiled=True).reshape(
        chans, local_rows, residues
    )
    normed_mid, scale_mid = layer_norm(regrouped.astype(jnp.float32), 0)
    mid_bf = normed_mid.astype(jnp.bfloat16)
    projected = jnp.einsum(
        "cij,cd->ijd", mid_bf, proj_weights[5], preferred_element_type=jnp.float32
    )
    gating = jax.nn.sigmoid(gate_pre)
    update = (gating * projected).astype(jnp.bfloat16)
    upstream = cotangent.astype(jnp.float32)
    gated_up = (upstream * gating).astype(jnp.bfloat16)
    gate_grad = (upstream * projected * gating * (1.0 - gating)).astype(jnp.bfloat16)
    out_weights = jnp.stack(
        [
            jnp.einsum("ikd,ikc->dc", normed_bf, gate_grad, preferred_element_type=jnp.float32),
            jnp.einsum("cij,ijd->cd", mid_bf, gated_up, preferred_element_type=jnp.float32),
        ]
    )
    mid_grad = jnp.einsum(
        "ijd,cd->cij", gated_up, proj_weights[5], preferred_element_type=jnp.float32
    )
    prod_grad = norm_backward(normed_mid, scale_mid, mid_grad, 0).astype(jnp.bfloat16)
    prod_grad = prod_grad.reshape(ranks, slab_width, local_rows, residues)
    slab_grad = lax.all_to_all(prod_grad, "rows", split_axis=0, concat_axis=2, tiled=True)
    left_part, right_part = edge_backward(slab_grad, left_held, right_held)
    left_back, right_back = (
        lax.all_to_all(left_part, "rows", split_axis=2, concat_axis=0, tiled=True),
        lax.all_to_all(right_part, "rows", split_axis=2, concat_axis=0, tiled=True),
    )
    left_full = left_back.reshape(chans, local_rows, residues).astype(jnp.float32)
    right_full = right_back.reshape(chans, local_rows, residues).astype(jnp.float32)
    edge_grad = jnp.stack(
        [
            left_full * left_sig,
            left_full * edge_pre[0] * left_sig * (1.0 - left_sig),
            right_full * right_sig,
            right_full * edge_pre[2] * right_sig * (1.0 - right_sig),
        ]
    ).astype(jnp.bfloat16)
    in_weights = jnp.einsum(
        "ikd,ncik->ndc", normed_bf, edge_grad, preferred_element_type=jnp.float32
    )
    input_grad = jnp.einsum(
        "ncik,ndc->ikd", edge_grad, proj_weights[0:4], preferred_element_type=jnp.float32
    )
    input_grad = input_grad + jnp.einsum(
        "ikc,dc->ikd", gate_grad, proj_weights[4], preferred_element_type=jnp.float32
    )
    pair_grad = norm_backward(normed_in, scale_in, input_grad, 2).astype(jnp.bfloat16)
    totals = lax.psum(
        jnp.concatenate([in_weights, out_weights], axis=0).astype(jnp.bfloat16), "rows"
    ).astype(jnp.float32)
    weight_grads = totals / residues
    return (update, pair_grad, weight_grads)


def solution(mesh):
    in_specs = (P(("groups", "rows"), None, None), P(), P(("groups", "rows"), None, None))
    out_specs = (
        P(("groups", "rows"), None, None),
        P(("groups", "rows"), None, None),
        P("groups", None, None),
    )
    return jax.shard_map(body, mesh=mesh, in_specs=in_specs, out_specs=out_specs, check_vma=False)
```

profile of v0, /device:TPU:0, one launch (start us, length us, event | category | flops | bytes accessed | tf_op | source)
XLA Modules:
  0.0 318.2 jit_solution(738744233146156121)
XLA Ops:
  7.2 1.5 copy.69
  11.7 2.0 copy-done
  14.8 7.4 %all-to-all-start.1 = ((bf16[16,8,16,256]{3,1,2,0:T(8,128)(2,1)}), bf16[16,8,16,256]{3,1,2,0:T(8,128)(2,1)S(1)}, u32[]{:S(2)}, u32[]{:S(2)}) async-start(bf16[16,8,16,256]{3,1,2,0:T(8,128)(2,1)} %copy.75), calls=%async_computation.1 | async-start | bytes 2097152 | tf_op jit(solution)/shard_map/all_to_all | solution.py:68
  23.3 21.9 %all-to-all-done.1 = bf16[16,8,16,256]{3,1,2,0:T(8,128)(2,1)S(1)} async-done(((bf16[16,8,16,256]{3,1,2,0:T(8,128)(2,1)}), bf16[16,8,16,256]{3,1,2,0:T(8,128)(2,1)S(1)}, u32[]{:S(2)}, u32[]{:S(2)}) %all-to-all-start.1) | async-done | bytes 1048608 | tf_op jit(solution)/shard_map/all_to_all | solution.py:68
  45.2 6.9 %all-to-all-start = ((bf16[16,8,16,256]{3,1,2,0:T(8,128)(2,1)}), bf16[16,8,16,256]{3,1,2,0:T(8,128)(2,1)}, u32[]{:S(2)}, u32[]{:S(2)}) async-start(bf16[16,8,16,256]{3,1,2,0:T(8,128)(2,1)} %copy.73), calls=%async_computation | async-start | bytes 2097152 | tf_op jit(solution)/shard_map/all_to_all | solution.py:67
  52.3 22.8 %all-to-all-done = bf16[16,8,16,256]{3,1,2,0:T(8,128)(2,1)} async-done(((bf16[16,8,16,256]{3,1,2,0:T(8,128)(2,1)}), bf16[16,8,16,256]{3,1,2,0:T(8,128)(2,1)}, u32[]{:S(2)}, u32[]{:S(2)}) %all-to-all-start) | async-done | bytes 1048608 | tf_op jit(solution)/shard_map/all_to_all | solution.py:67
  77.6 31.5 %all_to_all.72 = bf16[1,8,256,256]{3,1,0,2:T(8,128)(2,1)S(1)} all-to-all(bf16[1,8,256,256]{3,1,0,2:T(8,128)(2,1)S(1)} %copy.77), channel_id=1, replica_groups=mesh['groups'=2,'rows'=16] {'rows'}, dimensions={2} | all-to-all | bytes 2097152 | tf_op jit(solution)/shard_map/all_to_all | solution.py:71
  111.6 2.5 fusion.13
  114.1 1.6 bitcast_reduce_fusion
  115.8 1.6 fusion.47
  117.5 29.8 %all_to_all.73 = bf16[16,8,16,256]{3,1,2,0:T(8,128)(2,1)S(1)} all-to-all(bf16[16,8,16,256]{3,1,2,0:T(8,128)(2,1)S(1)} %copy.82), channel_id=1, replica_groups=mesh['groups'=2,'rows'=16] {'rows'}, dimensions={0} | all-to-all | bytes 2097152 | tf_op jit(solution)/shard_map/all_to_all | solution.py:95
  149.0 1.6 copy.84
  150.6 5.0 %all-to-all-start.4 = ((bf16[1,8,256,256]{3,1,0,2:T(8,128)(2,1)}), bf16[1,8,256,256]{3,1,0,2:T(8,128)(2,1)}, u32[]{:S(2)}, u32[]{:S(2)}) async-start(bf16[1,8,256,256]{3,1,0,2:T(8,128)(2,1)} %copy.84), calls=%async_computation.4 | async-start | bytes 2097152 | tf_op jit(solution)/shard_map/all_to_all | solution.py:98
  155.6 2.0 fusion.36
  157.7 1.6 copy.87
  159.3 19.3 %all-to-all-done.4 = bf16[1,8,256,256]{3,1,0,2:T(8,128)(2,1)} async-done(((bf16[1,8,256,256]{3,1,0,2:T(8,128)(2,1)}), bf16[1,8,256,256]{3,1,0,2:T(8,128)(2,1)}, u32[]{:S(2)}, u32[]{:S(2)}) %all-to-all-start.4) | async-done | bytes 1048608 | tf_op jit(solution)/shard_map/all_to_all | solution.py:98
  178.6 6.9 %all-to-all-start.5 = ((bf16[1,8,256,256]{3,1,0,2:T(8,128)(2,1)}), bf16[1,8,256,256]{3,1,0,2:T(8,128)(2,1)}, u32[]{:S(2)}, u32[]{:S(2)}) async-start(bf16[1,8,256,256]{3,1,0,2:T(8,128)(2,1)} %copy.87), calls=%async_computation.5 | async-start | bytes 2097152 | tf_op jit(solution)/shard_map/all_to_all | solution.py:99
  185.8 2.0 fusion.43
  187.8 2.9 fusion.42
  190.7 17.8 %all-to-all-done.5 = bf16[1,8,256,256]{3,1,0,2:T(8,128)(2,1)} async-done(((bf16[1,8,256,256]{3,1,0,2:T(8,128)(2,1)}), bf16[1,8,256,256]{3,1,0,2:T(8,128)(2,1)}, u32[]{:S(2)}, u32[]{:S(2)}) %all-to-all-start.5) | async-done | bytes 1048608 | tf_op jit(solution)/shard_map/all_to_all | solution.py:99
  208.5 5.0 %fusion.24 = (bf16[1,128,16,256]{3,1,0,2:T(8,128)(2,1)S(1)}, bf16[1,128,16,256]{3,1,0,2:T(8,128)(2,1)S(1)}, bf16[1,128,16,256]{3,1,0,2:T(8,128)(2,1)S(1)}, bf16[1,128,16,256]{3,1,0,2:T(8,128)(2,1)S(1)}) fusion(f32[4,128,16,256]{3,1,0,2:T(8,128)} %copy-done, bf16[1,8,16,16,256]{4,1,3,2,0:T(8,128)(2,1)} %bitcast.53, bf16[1,8,16,16,256]{4,1,3,2,0:T(8,128)(2,1)} %bitcast.51), kind=kLoop, calls=%fused_computation.37 | loop fusion | flops 11534336 | bytes 14680064 | tf_op jit(solution)/shard_map/convert.17
  217.5 1.6 fusion.8
  219.1 2.3 copy.93
  221.3 88.2 %all-reduce.2.cloned.1.call-done = bf16[6,128,128]{1,2,0:T(8,128)(2,1)} async-done(((bf16[6,128,128]{1,2,0:T(8,128)(2,1)}), bf16[6,128,128]{1,2,0:T(8,128)(2,1)}) %all-reduce.2.cloned.1.call-update) | async-done | bytes 196624 | tf_op jit(solution)/shard_map/psum | solution.py:121
  (53 shorter events, 18.1 us)
Async XLA Ops:
  7.2 2.1 copy-start.9
  10.5 3.2 %copy-start = (f32[4,128,16,256]{3,1,0,2:T(8,128)}, f32[4,128,16,256]{3,1,0,2:T(8,128)S(1)}, u32[]{:S(2)}) copy-start(f32[4,128,16,256]{3,1,0,2:T(8,128)S(1)} %convolution_bitcast_fusion) | copy-start | bytes 25165828
  14.8 30.3 %all-to-all-start.1 = ((bf16[16,8,16,256]{3,1,2,0:T(8,128)(2,1)}), bf16[16,8,16,256]{3,1,2,0:T(8,128)(2,1)S(1)}, u32[]{:S(2)}, u32[]{:S(2)}) async-start(bf16[16,8,16,256]{3,1,2,0:T(8,128)(2,1)} %copy.75), calls=%async_computation.1 | async-start | bytes 2097152 | tf_op jit(solution)/shard_map/all_to_all | solution.py:68
  45.2 29.9 %all-to-all-start = ((bf16[16,8,16,256]{3,1,2,0:T(8,128)(2,1)}), bf16[16,8,16,256]{3,1,2,0:T(8,128)(2,1)}, u32[]{:S(2)}, u32[]{:S(2)}) async-start(bf16[16,8,16,256]{3,1,2,0:T(8,128)(2,1)} %copy.73), calls=%async_computation | async-start | bytes 2097152 | tf_op jit(solution)/shard_map/all_to_all | solution.py:67
  52.3 24.7 %copy-start.2 = (bf16[1,8,16,16,256]{4,3,2,1,0:T(8,128)(2,1)}, bf16[1,8,16,16,256]{4,3,2,1,0:T(8,128)(2,1)S(1)}, u32[]{:S(2)}) copy-start(bf16[1,8,16,16,256]{4,3,2,1,0:T(8,128)(2,1)S(1)} %copy.76) | copy-start | bytes 3145732
  76.5 1.1 copy-start.1
  110.4 1.2 copy-start.7
  114.1 1.6 copy-start.5
  117.5 31.0 %copy-start.3 = (bf16[1,8,16,16,256]{4,3,2,1,0:T(8,128)(2,1)S(1)}, bf16[1,8,16,16,256]{4,3,2,1,0:T(8,128)(2,1)}, u32[]{:S(2)}) copy-start(bf16[1,8,16,16,256]{4,3,2,1,0:T(8,128)(2,1)} %copy-done.2) | copy-start | bytes 3145732
  147.3 1.0 copy-start.4
  150.6 28.0 %all-to-all-start.4 = ((bf16[1,8,256,256]{3,1,0,2:T(8,128)(2,1)}), bf16[1,8,256,256]{3,1,0,2:T(8,128)(2,1)}, u32[]{:S(2)}, u32[]{:S(2)}) async-start(bf16[1,8,256,256]{3,1,0,2:T(8,128)(2,1)} %copy.84), calls=%async_computation.4 | async-start | bytes 2097152 | tf_op jit(solution)/shard_map/all_to_all | solution.py:98
  178.6 29.9 %all-to-all-start.5 = ((bf16[1,8,256,256]{3,1,0,2:T(8,128)(2,1)}), bf16[1,8,256,256]{3,1,0,2:T(8,128)(2,1)}, u32[]{:S(2)}, u32[]{:S(2)}) async-start(bf16[1,8,256,256]{3,1,0,2:T(8,128)(2,1)} %copy.87), calls=%async_computation.5 | async-start | bytes 2097152 | tf_op jit(solution)/shard_map/all_to_all | solution.py:99
  185.5 124.0 %all-reduce.2.cloned.1.call-start = ((), (), s32[]{:S(2)}) async-start(), calls=%async_computation.6 | async-start | bytes 393216 | tf_op jit(solution)/shard_map/psum | solution.py:121
  185.8 2.0 copy-start.6
  214.8 1.2 copy-start.8
Sparse Core Ops, SparseCore 0:
  217.6 91.8 all-reduce.1
where the time goes:
time: 319 us; the launch traced here: 318 us
  waiting for transfers between devices  170 us (53%)
  blocking collectives  61.3 us (19%)
  starting transfers between devices  26.5 us (8%)
  local copies, waits for them, and re-layouts  16.9 us (5%)
  matrix products  16.5 us (5%)
  between operations  14.4 us (5%)
  other arithmetic  12.6 us (4%)
    psum x1, waiting for transfers between devices, body(): lax.psum(jnp.concatenate([in_weights, out_weights], axis=0).astype(jnp.bf...  88.2 us
    all_to_all x1, blocking collectives, body(): lax.all_to_all(products, 'rows', split_axis=2, concat_axis=0, tiled=True)  31.5 us
    all_to_all x1, blocking collectives, body(): lax.all_to_all(prod_grad, 'rows', split_axis=0, concat_axis=2, tiled=True)  29.8 us
    all_to_all x1, waiting for transfers between devices, body(): lax.all_to_all(left_edge, 'rows', split_axis=0, concat_axis=2, tiled=True)  22.8 us
    all_to_all x1, waiting for transfers between devices, body(): lax.all_to_all(right_edge, 'rows', split_axis=0, concat_axis=2, tiled=True)  21.9 us
    all_to_all x1, waiting for transfers between devices, body(): lax.all_to_all(left_part, 'rows', split_axis=2, concat_axis=0, tiled=True)  19.3 us
    all_to_all x1, waiting for transfers between devices, body(): lax.all_to_all(right_part, 'rows', split_axis=2, concat_axis=0, tiled=True)  17.8 us
    unnamed x23, local copies, waits for them, and re-layouts  8.91 us
  transfers between devices with their start and end apart: 5, of which 5 were waited for; matrix products, arithmetic and copies ran while one was open for 4% of the time, Pallas kernels for 0%

commit v1 on v0

--- a/solution.py
+++ b/solution.py
@@ -2,6 +2,29 @@
 import jax.numpy as jnp
 from jax import lax
 from jax.sharding import PartitionSpec as P
+
+
+def cut_along(shard, dim, count):
+    shape = shard.shape
+    tiles = shard.reshape(*shape[:dim], count, shape[dim] // count, *shape[dim + 1 :])
+    return jnp.moveaxis(tiles, dim, 0)
+
+
+def joined_along(pieces, dim):
+    pieces = jnp.moveaxis(pieces, 0, dim)
+    dims = pieces.shape
+    return pieces.reshape(*dims[:dim], dims[dim] * dims[dim + 1], *dims[dim + 2 :])
+
+
+def sent_to_each(x, axis, split_dim, concat_dim):
+    size, position = (lax.axis_size(axis), lax.axis_index(axis))
+    blocks = cut_along(x, split_dim, size)
+    done = [blocks[position]]
+    for step in range(1, size):
+        sent = blocks[(position + step) % size]
+        done.append(lax.ppermute(sent, axis, [(i, (i + step) % size) for i in range(size)]))
+    blocks = jnp.stack(done)[(position - jnp.arange(size)) % size]
+    return joined_along(blocks, concat_dim)
 
 
 def layer_norm(values, along_dim):
@@ -95,7 +118,7 @@
     slab_grad = lax.all_to_all(prod_grad, "rows", split_axis=0, concat_axis=2, tiled=True)
     left_part, right_part = edge_backward(slab_grad, left_held, right_held)
     left_back, right_back = (
-        lax.all_to_all(left_part, "rows", split_axis=2, concat_axis=0, tiled=True),
+        sent_to_each(left_part, "rows", 2, 0),
         lax.all_to_all(right_part, "rows", split_axis=2, concat_axis=0, tiled=True),
     )
     left_full = left_back.reshape(chans, local_rows, residues).astype(jnp.float32)

time: 319 us -> 353 us (1.11)
  waiting for transfers between devices: 170 us -> 220 us
  blocking collectives: 61.3 us -> 31.5 us
  starting transfers between devices: 26.5 us -> 36.5 us
    ppermute x0 -> x15, waiting for transfers between devices: none -> 68.2 us  [sent_to_each(): lax.ppermute(sent, axis, [(i, (i + step) % size) for i in range(size)])]
    all_to_all x1 -> x0, blocking collectives: 29.8 us -> none  [body(): lax.all_to_all(prod_grad, 'rows', split_axis=0, concat_axis=2, tiled=True)]
    all_to_all x1, waiting for transfers between devices: 17.8 us -> 0.01 us  [body(): lax.all_to_all(right_part, 'rows', split_axis=2, concat_axis=0, tiled=True)]
    ppermute x0 -> x15, starting transfers between devices: none -> 10.2 us  [sent_to_each(): lax.ppermute(sent, axis, [(i, (i + step) % size) for i in range(size)])]
    unnamed x23 -> x36, local copies, waits for them, and re-layouts: 8.91 us -> 8.01 us
  transfers between devices with their start and end apart: 5 -> 20, of which waited for: 5 -> 15; matrix products, arithmetic and copies ran while one was open for 4% -> 4% of each run, Pallas kernels for 0% -> 0%
where the time goes in v1:
time: 353 us; the launch traced here: 352 us
  waiting for transfers between devices  220 us (62%)
  starting transfers between devices  36.5 us (10%)
  blocking collectives  31.5 us (9%)
  local copies, waits for them, and re-layouts  18.4 us (5%)
  matrix products  16.5 us (5%)
  other arithmetic  14.8 us (4%)
  between operations  14.7 us (4%)
    psum x1, waiting for transfers between devices, body(): lax.psum(jnp.concatenate([in_weights, out_weights], axis=0).astype(jnp.bf...  89.2 us
    ppermute x15, waiting for transfers between devices, sent_to_each(): lax.ppermute(sent, axis, [(i, (i + step) % size) for i in range(size)])  68.2 us
    all_to_all x1, blocking collectives, body(): lax.all_to_all(products, 'rows', split_axis=2, concat_axis=0, tiled=True)  31.5 us
    all_to_all x1, waiting for transfers between devices, body(): lax.all_to_all(left_edge, 'rows', split_axis=0, concat_axis=2, tiled=True)  22.8 us
    all_to_all x1, waiting for transfers between devices, body(): lax.all_to_all(right_edge, 'rows', split_axis=0, concat_axis=2, tiled=True)  21.9 us
    all_to_all x1, waiting for transfers between devices, body(): lax.all_to_all(prod_grad, 'rows', split_axis=0, concat_axis=2, tiled=True)  17.9 us
    ppermute x15, starting transfers between devices, sent_to_each(): lax.ppermute(sent, axis, [(i, (i + step) % size) for i in range(size)])  10.2 us
    unnamed x36, local copies, waits for them, and re-layouts  8.01 us
  transfers between devices with their start and end apart: 20, of which 15 were waited for; matrix products, arithmetic and copies ran while one was open for 4% of the time, Pallas kernels for 0%

profile of v1, /device:TPU:0, one launch (start us, length us, event | category | flops | bytes accessed | tf_op | source)
XLA Modules:
  0.0 352.3 jit_solution(3924180620490038080)
XLA Ops:
  14.8 7.4 %all-to-all-start.1 = ((bf16[16,8,16,256]{3,1,2,0:T(8,128)(2,1)}), bf16[16,8,16,256]{3,1,2,0:T(8,128)(2,1)S(1)}, u32[]{:S(2)}, u32[]{:S(2)}) async-start(bf16[16,8,16,256]{3,1,2,0:T(8,128)(2,1)} %copy.73), calls=%async_computation.1 | async-start | bytes 2097152 | tf_op jit(solution)/shard_map/all_to_all | solution.py:91
  23.3 21.9 %all-to-all-done.1 = bf16[16,8,16,256]{3,1,2,0:T(8,128)(2,1)S(1)} async-done(((bf16[16,8,16,256]{3,1,2,0:T(8,128)(2,1)}), bf16[16,8,16,256]{3,1,2,0:T(8,128)(2,1)S(1)}, u32[]{:S(2)}, u32[]{:S(2)}) %all-to-all-start.1) | async-done | bytes 1048608 | tf_op jit(solution)/shard_map/all_to_all | solution.py:91
  45.2 6.9 %all-to-all-start = ((bf16[16,8,16,256]{3,1,2,0:T(8,128)(2,1)}), bf16[16,8,16,256]{3,1,2,0:T(8,128)(2,1)}, u32[]{:S(2)}, u32[]{:S(2)}) async-start(bf16[16,8,16,256]{3,1,2,0:T(8,128)(2,1)} %copy.71), calls=%async_computation | async-start | bytes 2097152 | tf_op jit(solution)/shard_map/all_to_all | solution.py:90
  52.3 22.8 %all-to-all-done = bf16[16,8,16,256]{3,1,2,0:T(8,128)(2,1)} async-done(((bf16[16,8,16,256]{3,1,2,0:T(8,128)(2,1)}), bf16[16,8,16,256]{3,1,2,0:T(8,128)(2,1)}, u32[]{:S(2)}, u32[]{:S(2)}) %all-to-all-start) | async-done | bytes 1048608 | tf_op jit(solution)/shard_map/all_to_all | solution.py:90
  77.6 31.5 %all_to_all.63 = bf16[1,8,256,256]{3,1,0,2:T(8,128)(2,1)S(1)} all-to-all(bf16[1,8,256,256]{3,1,0,2:T(8,128)(2,1)S(1)} %copy.75), channel_id=1, replica_groups=mesh['groups'=2,'rows'=16] {'rows'}, dimensions={2} | all-to-all | bytes 2097152 | tf_op jit(solution)/shard_map/all_to_all | solution.py:94
  111.6 2.5 fusion.13
  118.5 5.0 %all-to-all-start.3 = ((bf16[16,8,16,256]{3,1,2,0:T(8,128)(2,1)}), bf16[16,8,16,256]{3,1,2,0:T(8,128)(2,1)}, u32[]{:S(2)}, u32[]{:S(2)}) async-start(bf16[16,8,16,256]{3,1,2,0:T(8,128)(2,1)} %copy.80), calls=%async_computation.3 | async-start | bytes 2097152 | tf_op jit(solution)/shard_map/all_to_all | solution.py:118
  125.8 2.9 fusion.41
  128.7 17.9 %all-to-all-done.3 = bf16[16,8,16,256]{3,1,2,0:T(8,128)(2,1)} async-done(((bf16[16,8,16,256]{3,1,2,0:T(8,128)(2,1)}), bf16[16,8,16,256]{3,1,2,0:T(8,128)(2,1)}, u32[]{:S(2)}, u32[]{:S(2)}) %all-to-all-start.3) | async-done | bytes 1048608 | tf_op jit(solution)/shard_map/all_to_all | solution.py:118
  152.2 6.9 %all-to-all-start.4 = ((bf16[1,8,256,256]{3,1,0,2:T(8,128)(2,1)}), bf16[1,8,256,256]{3,1,0,2:T(8,128)(2,1)}, u32[]{:S(2)}, u32[]{:S(2)}) async-start(bf16[1,8,256,256]{3,1,0,2:T(8,128)(2,1)} %copy.84), calls=%async_computation.4 | async-start | bytes 2097152 | tf_op jit(solution)/shard_map/all_to_all | solution.py:122
  159.3 4.4 %collective-permute-start.14 = (bf16[1,8,16,256]{3,2,1,0:T(8,128)(2,1)S(1)}, bf16[1,8,16,256]{3,2,1,0:T(8,128)(2,1)S(1)}, u32[]{:S(2)}, u32[]{:S(2)}) collective-permute-start(bf16[1,8,16,256]{3,2,1,0:T(8,128)(2,1)S(1)} %get-tuple-element.29), channel_id=1, source_target_pairs={{0,15},{1,0},{2,1},{3,2},{4,3},{5,4},{6,5},{7,6},{8,7},{9,8},{10,9... | collective-permute-start | bytes 196616 | tf_op jit(solution)/shard_map/ppermute | solution.py:25
  166.1 18.1 %collective-permute-done = bf16[1,8,16,256]{3,2,1,0:T(8,128)(2,1)S(1)} collective-permute-done((bf16[1,8,16,256]{3,2,1,0:T(8,128)(2,1)S(1)}, bf16[1,8,16,256]{3,2,1,0:T(8,128)(2,1)S(1)}, u32[]{:S(2)}, u32[]{:S(2)}) %collective-permute-start) | collective-permute-done | bytes 65568 | tf_op jit(solution)/shard_map/ppermute | solution.py:25
  184.2 7.0 %collective-permute-done.1 = bf16[1,8,16,256]{3,2,1,0:T(8,128)(2,1)S(1)} collective-permute-done((bf16[1,8,16,256]{3,2,1,0:T(8,128)(2,1)S(1)}, bf16[1,8,16,256]{3,2,1,0:T(8,128)(2,1)S(1)}, u32[]{:S(2)}, u32[]{:S(2)}) %collective-permute-start.1) | collective-permute-done | bytes 65568 | tf_op jit(solution)/shard_map/ppermute | solution.py:25
  191.2 5.5 %collective-permute-done.2 = bf16[1,8,16,256]{3,2,1,0:T(8,128)(2,1)S(1)} collective-permute-done((bf16[1,8,16,256]{3,2,1,0:T(8,128)(2,1)S(1)}, bf16[1,8,16,256]{3,2,1,0:T(8,128)(2,1)S(1)}, u32[]{:S(2)}, u32[]{:S(2)}) %collective-permute-start.2) | collective-permute-done | bytes 65568 | tf_op jit(solution)/shard_map/ppermute | solution.py:25
  196.7 6.1 %collective-permute-done.3 = bf16[1,8,16,256]{3,2,1,0:T(8,128)(2,1)S(1)} collective-permute-done((bf16[1,8,16,256]{3,2,1,0:T(8,128)(2,1)S(1)}, bf16[1,8,16,256]{3,2,1,0:T(8,128)(2,1)S(1)}, u32[]{:S(2)}, u32[]{:S(2)}) %collective-permute-start.3) | collective-permute-done | bytes 65568 | tf_op jit(solution)/shard_map/ppermute | solution.py:25
  202.7 5.5 %collective-permute-done.4 = bf16[1,8,16,256]{3,2,1,0:T(8,128)(2,1)S(1)} collective-permute-done((bf16[1,8,16,256]{3,2,1,0:T(8,128)(2,1)S(1)}, bf16[1,8,16,256]{3,2,1,0:T(8,128)(2,1)S(1)}, u32[]{:S(2)}, u32[]{:S(2)}) %collective-permute-start.4) | collective-permute-done | bytes 65568 | tf_op jit(solution)/shard_map/ppermute | solution.py:25
  208.2 6.1 %collective-permute-done.5 = bf16[1,8,16,256]{3,2,1,0:T(8,128)(2,1)S(1)} collective-permute-done((bf16[1,8,16,256]{3,2,1,0:T(8,128)(2,1)S(1)}, bf16[1,8,16,256]{3,2,1,0:T(8,128)(2,1)S(1)}, u32[]{:S(2)}, u32[]{:S(2)}) %collective-permute-start.5) | collective-permute-done | bytes 65568 | tf_op jit(solution)/shard_map/ppermute | solution.py:25
  214.3 4.9 %collective-permute-done.6 = bf16[1,8,16,256]{3,2,1,0:T(8,128)(2,1)S(1)} collective-permute-done((bf16[1,8,16,256]{3,2,1,0:T(8,128)(2,1)S(1)}, bf16[1,8,16,256]{3,2,1,0:T(8,128)(2,1)S(1)}, u32[]{:S(2)}, u32[]{:S(2)}) %collective-permute-start.6) | collective-permute-done | bytes 65568 | tf_op jit(solution)/shard_map/ppermute | solution.py:25
  219.6 4.7 %collective-permute-done.7 = bf16[1,8,16,256]{3,2,1,0:T(8,128)(2,1)S(1)} collective-permute-done((bf16[1,8,16,256]{3,2,1,0:T(8,128)(2,1)S(1)}, bf16[1,8,16,256]{3,2,1,0:T(8,128)(2,1)S(1)}, u32[]{:S(2)}, u32[]{:S(2)}) %collective-permute-start.7) | collective-permute-done | bytes 65568 | tf_op jit(solution)/shard_map/ppermute | solution.py:25
  224.3 4.6 %collective-permute-done.8 = bf16[1,8,16,256]{3,2,1,0:T(8,128)(2,1)S(1)} collective-permute-done((bf16[1,8,16,256]{3,2,1,0:T(8,128)(2,1)S(1)}, bf16[1,8,16,256]{3,2,1,0:T(8,128)(2,1)S(1)}, u32[]{:S(2)}, u32[]{:S(2)}) %collective-permute-start.8) | collective-permute-done | bytes 65568 | tf_op jit(solution)/shard_map/ppermute | solution.py:25
  230.7 3.4 collective-permute-done.9
  235.3 2.5 collective-permute-done.10
  241.0 5.7 %fusion.24 = (bf16[1,128,16,256]{3,1,0,2:T(8,128)(2,1)S(1)}, bf16[1,128,16,256]{3,1,0,2:T(8,128)(2,1)S(1)}, bf16[1,128,16,256]{3,1,0,2:T(8,128)(2,1)S(1)}, bf16[1,128,16,256]{3,1,0,2:T(8,128)(2,1)S(1)}) fusion(f32[16,8,16,256]{3,2,1,0:T(8,128)S(1)} %convert_element_type.155, f32[4,128,16,256]{3,1,0,2:T(8,128)} %copy-done, ...), kind=kLoop, calls=%fused_computation.38 | loop fusion | flops 11010048 | bytes 15728640 | tf_op jit(solution)/shard_map/convert.15
  254.4 89.2 %all-reduce.2.cloned.1.call-done = bf16[6,128,128]{1,2,0:T(8,128)(2,1)} async-done(((bf16[6,128,128]{1,2,0:T(8,128)(2,1)}), bf16[6,128,128]{1,2,0:T(8,128)(2,1)}) %all-reduce.2.cloned.1.call-update) | async-done | bytes 196624 | tf_op jit(solution)/shard_map/psum | solution.py:144
  (100 shorter events, 44.5 us)
Async XLA Ops:
  7.2 2.1 copy-start.8
  10.5 3.2 copy-start
  14.8 30.3 %all-to-all-start.1 = ((bf16[16,8,16,256]{3,1,2,0:T(8,128)(2,1)}), bf16[16,8,16,256]{3,1,2,0:T(8,128)(2,1)S(1)}, u32[]{:S(2)}, u32[]{:S(2)}) async-start(bf16[16,8,16,256]{3,1,2,0:T(8,128)(2,1)} %copy.73), calls=%async_computation.1 | async-start | bytes 2097152 | tf_op jit(solution)/shard_map/all_to_all | solution.py:91
  45.2 29.9 %all-to-all-start = ((bf16[16,8,16,256]{3,1,2,0:T(8,128)(2,1)}), bf16[16,8,16,256]{3,1,2,0:T(8,128)(2,1)}, u32[]{:S(2)}, u32[]{:S(2)}) async-start(bf16[16,8,16,256]{3,1,2,0:T(8,128)(2,1)} %copy.71), calls=%async_computation | async-start | bytes 2097152 | tf_op jit(solution)/shard_map/all_to_all | solution.py:90
  52.3 24.7 %copy-start.1 = (bf16[1,8,16,16,256]{4,3,2,1,0:T(8,128)(2,1)}, bf16[1,8,16,16,256]{4,3,2,1,0:T(8,128)(2,1)S(1)}, u32[]{:S(2)}) copy-start(bf16[1,8,16,16,256]{4,3,2,1,0:T(8,128)(2,1)S(1)} %copy.74) | copy-start | bytes 3145732
  118.5 28.0 %all-to-all-start.3 = ((bf16[16,8,16,256]{3,1,2,0:T(8,128)(2,1)}), bf16[16,8,16,256]{3,1,2,0:T(8,128)(2,1)}, u32[]{:S(2)}, u32[]{:S(2)}) async-start(bf16[16,8,16,256]{3,1,2,0:T(8,128)(2,1)} %copy.80), calls=%async_computation.3 | async-start | bytes 2097152 | tf_op jit(solution)/shard_map/all_to_all | solution.py:118
  148.6 3.1 copy-start.2
  152.2 88.8 %all-to-all-start.4 = ((bf16[1,8,256,256]{3,1,0,2:T(8,128)(2,1)}), bf16[1,8,256,256]{3,1,0,2:T(8,128)(2,1)}, u32[]{:S(2)}, u32[]{:S(2)}) async-start(bf16[1,8,256,256]{3,1,0,2:T(8,128)(2,1)} %copy.84), calls=%async_computation.4 | async-start | bytes 2097152 | tf_op jit(solution)/shard_map/all_to_all | solution.py:122
  159.1 184.5 %all-reduce.2.cloned.1.call-start = ((), (), s32[]{:S(2)}) async-start(), calls=%async_computation.5 | async-start | bytes 393216 | tf_op jit(solution)/shard_map/psum | solution.py:144
  159.3 78.5 %collective-permute-start.14 = (bf16[1,8,16,256]{3,2,1,0:T(8,128)(2,1)S(1)}, bf16[1,8,16,256]{3,2,1,0:T(8,128)(2,1)S(1)}, u32[]{:S(2)}, u32[]{:S(2)}) collective-permute-start(bf16[1,8,16,256]{3,2,1,0:T(8,128)(2,1)S(1)} %get-tuple-element.29), channel_id=1, source_target_pairs={{0,15},{1,0},{2,1},{3,2},{4,3},{5,4},{6,5},{7,6},{8,7},{9,8},{10,9... | collective-permute-start | bytes 196616 | tf_op jit(solution)/shard_map/ppermute | solution.py:25
  163.7 74.1 %collective-permute-start.13 = (bf16[1,8,16,256]{3,2,1,0:T(8,128)(2,1)S(1)}, bf16[1,8,16,256]{3,2,1,0:T(8,128)(2,1)S(1)}, u32[]{:S(2)}, u32[]{:S(2)}) collective-permute-start(bf16[1,8,16,256]{3,2,1,0:T(8,128)(2,1)S(1)} %get-tuple-element.30), channel_id=1, source_target_pairs={{0,14},{1,15},{2,0},{3,1},{4,2},{5,3},{6,4},{7,5},{8,6},{9,7},{10,... | collective-permute-start | bytes 196616 | tf_op jit(solution)/shard_map/ppermute | solution.py:25
  164.2 73.6 %collective-permute-start.12 = (bf16[1,8,16,256]{3,2,1,0:T(8,128)(2,1)S(1)}, bf16[1,8,16,256]{3,2,1,0:T(8,128)(2,1)S(1)}, u32[]{:S(2)}, u32[]{:S(2)}) collective-permute-start(bf16[1,8,16,256]{3,2,1,0:T(8,128)(2,1)S(1)} %get-tuple-element.31), channel_id=1, source_target_pairs={{0,13},{1,14},{2,15},{3,0},{4,1},{5,2},{6,3},{7,4},{8,5},{9,6},{10... | collective-permute-start | bytes 196616 | tf_op jit(solution)/shard_map/ppermute | solution.py:25
  164.3 73.5 %collective-permute-start.11 = (bf16[1,8,16,256]{3,2,1,0:T(8,128)(2,1)S(1)}, bf16[1,8,16,256]{3,2,1,0:T(8,128)(2,1)S(1)}, u32[]{:S(2)}, u32[]{:S(2)}) collective-permute-start(bf16[1,8,16,256]{3,2,1,0:T(8,128)(2,1)S(1)} %get-tuple-element.32), channel_id=1, source_target_pairs={{0,12},{1,13},{2,14},{3,15},{4,0},{5,1},{6,2},{7,3},{8,4},{9,5},{1... | collective-permute-start | bytes 196616 | tf_op jit(solution)/shard_map/ppermute | solution.py:25
  164.9 19.3 %collective-permute-start = (bf16[1,8,16,256]{3,2,1,0:T(8,128)(2,1)S(1)}, bf16[1,8,16,256]{3,2,1,0:T(8,128)(2,1)S(1)}, u32[]{:S(2)}, u32[]{:S(2)}) collective-permute-start(bf16[1,8,16,256]{3,2,1,0:T(8,128)(2,1)S(1)} %get-tuple-element.43), channel_id=1, source_target_pairs={{0,1},{1,2},{2,3},{3,4},{4,5},{5,6},{6,7},{7,8},{8,9},{9,10},{10,1... | collective-permute-start | bytes 196616 | tf_op jit(solution)/shard_map/ppermute | solution.py:25
  184.2 7.0 %collective-permute-start.1 = (bf16[1,8,16,256]{3,2,1,0:T(8,128)(2,1)S(1)}, bf16[1,8,16,256]{3,2,1,0:T(8,128)(2,1)S(1)}, u32[]{:S(2)}, u32[]{:S(2)}) collective-permute-start(bf16[1,8,16,256]{3,2,1,0:T(8,128)(2,1)S(1)} %get-tuple-element.42), channel_id=1, source_target_pairs={{0,2},{1,3},{2,4},{3,5},{4,6},{5,7},{6,8},{7,9},{8,10},{9,11},{10,... | collective-permute-start | bytes 196616 | tf_op jit(solution)/shard_map/ppermute | solution.py:25
  191.2 5.5 %collective-permute-start.2 = (bf16[1,8,16,256]{3,2,1,0:T(8,128)(2,1)S(1)}, bf16[1,8,16,256]{3,2,1,0:T(8,128)(2,1)S(1)}, u32[]{:S(2)}, u32[]{:S(2)}) collective-permute-start(bf16[1,8,16,256]{3,2,1,0:T(8,128)(2,1)S(1)} %get-tuple-element.41), channel_id=1, source_target_pairs={{0,3},{1,4},{2,5},{3,6},{4,7},{5,8},{6,9},{7,10},{8,11},{9,12},{10... | collective-permute-start | bytes 196616 | tf_op jit(solution)/shard_map/ppermute | solution.py:25
  196.7 6.1 %collective-permute-start.3 = (bf16[1,8,16,256]{3,2,1,0:T(8,128)(2,1)S(1)}, bf16[1,8,16,256]{3,2,1,0:T(8,128)(2,1)S(1)}, u32[]{:S(2)}, u32[]{:S(2)}) collective-permute-start(bf16[1,8,16,256]{3,2,1,0:T(8,128)(2,1)S(1)} %get-tuple-element.40), channel_id=1, source_target_pairs={{0,4},{1,5},{2,6},{3,7},{4,8},{5,9},{6,10},{7,11},{8,12},{9,13},{1... | collective-permute-start | bytes 196616 | tf_op jit(solution)/shard_map/ppermute | solution.py:25
  202.7 5.5 %collective-permute-start.4 = (bf16[1,8,16,256]{3,2,1,0:T(8,128)(2,1)S(1)}, bf16[1,8,16,256]{3,2,1,0:T(8,128)(2,1)S(1)}, u32[]{:S(2)}, u32[]{:S(2)}) collective-permute-start(bf16[1,8,16,256]{3,2,1,0:T(8,128)(2,1)S(1)} %get-tuple-element.39), channel_id=1, source_target_pairs={{0,5},{1,6},{2,7},{3,8},{4,9},{5,10},{6,11},{7,12},{8,13},{9,14},{... | collective-permute-start | bytes 196616 | tf_op jit(solution)/shard_map/ppermute | solution.py:25
  208.2 6.1 %collective-permute-start.5 = (bf16[1,8,16,256]{3,2,1,0:T(8,128)(2,1)S(1)}, bf16[1,8,16,256]{3,2,1,0:T(8,128)(2,1)S(1)}, u32[]{:S(2)}, u32[]{:S(2)}) collective-permute-start(bf16[1,8,16,256]{3,2,1,0:T(8,128)(2,1)S(1)} %get-tuple-element.38), channel_id=1, source_target_pairs={{0,6},{1,7},{2,8},{3,9},{4,10},{5,11},{6,12},{7,13},{8,14},{9,15},... | collective-permute-start | bytes 196616 | tf_op jit(solution)/shard_map/ppermute | solution.py:25
  214.3 4.9 %collective-permute-start.6 = (bf16[1,8,16,256]{3,2,1,0:T(8,128)(2,1)S(1)}, bf16[1,8,16,256]{3,2,1,0:T(8,128)(2,1)S(1)}, u32[]{:S(2)}, u32[]{:S(2)}) collective-permute-start(bf16[1,8,16,256]{3,2,1,0:T(8,128)(2,1)S(1)} %get-tuple-element.37), channel_id=1, source_target_pairs={{0,7},{1,8},{2,9},{3,10},{4,11},{5,12},{6,13},{7,14},{8,15},{9,0},... | collective-permute-start | bytes 196616 | tf_op jit(solution)/shard_map/ppermute | solution.py:25
  219.1 5.2 %collective-permute-start.7 = (bf16[1,8,16,256]{3,2,1,0:T(8,128)(2,1)S(1)}, bf16[1,8,16,256]{3,2,1,0:T(8,128)(2,1)S(1)}, u32[]{:S(2)}, u32[]{:S(2)}) collective-permute-start(bf16[1,8,16,256]{3,2,1,0:T(8,128)(2,1)S(1)} %get-tuple-element.36), channel_id=1, source_target_pairs={{0,8},{1,9},{2,10},{3,11},{4,12},{5,13},{6,14},{7,15},{8,0},{9,1},... | collective-permute-start | bytes 196616 | tf_op jit(solution)/shard_map/ppermute | solution.py:25
  224.3 4.6 %collective-permute-start.8 = (bf16[1,8,16,256]{3,2,1,0:T(8,128)(2,1)S(1)}, bf16[1,8,16,256]{3,2,1,0:T(8,128)(2,1)S(1)}, u32[]{:S(2)}, u32[]{:S(2)}) collective-permute-start(bf16[1,8,16,256]{3,2,1,0:T(8,128)(2,1)S(1)} %get-tuple-element.35), channel_id=1, source_target_pairs={{0,9},{1,10},{2,11},{3,12},{4,13},{5,14},{6,15},{7,0},{8,1},{9,2},... | collective-permute-start | bytes 196616 | tf_op jit(solution)/shard_map/ppermute | solution.py:25
  228.9 5.2 %collective-permute-start.9 = (bf16[1,8,16,256]{3,2,1,0:T(8,128)(2,1)S(1)}, bf16[1,8,16,256]{3,2,1,0:T(8,128)(2,1)S(1)}, u32[]{:S(2)}, u32[]{:S(2)}) collective-permute-start(bf16[1,8,16,256]{3,2,1,0:T(8,128)(2,1)S(1)} %get-tuple-element.34), channel_id=1, source_target_pairs={{0,10},{1,11},{2,12},{3,13},{4,14},{5,15},{6,0},{7,1},{8,2},{9,3},... | collective-permute-start | bytes 196616 | tf_op jit(solution)/shard_map/ppermute | solution.py:25
  234.1 3.7 %collective-permute-start.10 = (bf16[1,8,16,256]{3,2,1,0:T(8,128)(2,1)S(1)}, bf16[1,8,16,256]{3,2,1,0:T(8,128)(2,1)S(1)}, u32[]{:S(2)}, u32[]{:S(2)}) collective-permute-start(bf16[1,8,16,256]{3,2,1,0:T(8,128)(2,1)S(1)} %get-tuple-element.33), channel_id=1, source_target_pairs={{0,11},{1,12},{2,13},{3,14},{4,15},{5,0},{6,1},{7,2},{8,3},{9,4},{... | collective-permute-start | bytes 196616 | tf_op jit(solution)/shard_map/ppermute | solution.py:25
  (5 other events, 7.2 us)
Sparse Core Ops, SparseCore 0:
  250.7 92.8 all-reduce.1
